TPU v7x, 32 devices: a whole 2x2x4 slice. The times are simulated.
32 devices in a mesh: groups: 2 (over y), query: 4 (over z), proj: 4 (over x, core).
Axes of the slice: x: 2, y: 2, z: 4, core: 2. Of those that a mesh axis runs over, the one named last changes fastest.
Arguments:
- query_feats: float32 [4096, 8192], P(('groups', 'query'), 'proj'), parts along dimension 0, may hold values from -6 to 6
- train_feats: float32 [2048, 8192], P(('groups', 'query'), 'proj'), parts along dimension 0, may hold values from -0.0625 to 0.0625
- out_weight: float32 [2048], P(('groups', 'proj')), parts along dimension 0, may hold values from 0.05 to 1
Outputs:
- scores: float32 [2048, 2048], P(('groups', 'proj'), 'query'), parts along dimension 0
There are 2 independent parts, one for each index of `groups`. A program takes and returns all parts, laid end to end along the dimension named above; each array names one. Nothing has to cross between parts.
All inputs are finite; a program needn't handle non-finite values.
Results may differ from a plain program's by a relative error of at most 0.000078.
Values sent between devices are 32-bit elements; how exact they have to be, the bound alone decides.
A program may use at most 128 MiB of HBM per device.

v0:
```python
import jax
import jax.numpy as jnp
from jax import lax
from jax.sharding import PartitionSpec as P


def body(query_feats, train_feats, out_weight):
    terms = lax.dot_general(
        lax.all_gather(train_feats, "query", axis=0, tiled=True),
        query_feats,
        (((1,), (1,)), ((), ())),
        precision=lax.Precision.HIGHEST,
        preferred_element_type=jnp.float32,
    )
    total = lax.psum(terms, "proj")
    own_rows = terms.shape[0] // lax.axis_size("proj")
    mine = lax.dynamic_slice_in_dim(total, lax.axis_index("proj") * own_rows, own_rows, 0)
    return mine * out_weight[:, None]


def solution(mesh):
    placed = (P(("groups", "query"), "proj"), P(("groups", "query"), "proj"), P(("groups", "proj")))
    return jax.shard_map(
        body, mesh=mesh, in_specs=placed, out_specs=P(("groups", "proj"), "query"), check_vma=False
    )
```

profile of v0, /device:TPU:0, one launch (start us, length us, event | category | flops | bytes accessed | tf_op | source)
XLA Modules:
  0.0 237.0 jit_solution(8123800469763578970)
XLA Ops:
  6.5 0.0 all-gather.2.cloned.1.call-start
  6.5 0.7 all-gather.2.cloned.1.call-update
  7.3 0.0 copy-start
  7.3 0.0 all-reduce.2.cloned.1.call-start
  7.3 154.0 %all-gather.2.cloned.1.call-done = f32[1024,2048]{1,0:T(8,128)} async-done(((f32[256,2048]{1,0:T(8,128)}), f32[1024,2048]{1,0:T(8,128)}) %all-gather.2.cloned.1.call-update) | async-done | bytes 8388624 | tf_op jit(solution)/shard_map/all_gather | solution.py:9
  161.3 17.1 %fusion = f32[1024,512]{1,0:T(8,128)} fusion(f32[1024,2048]{1,0:T(8,128)} %all-gather.2.cloned.1.call-done, f32[512,2048]{1,0:T(8,128)} %param.3), kind=kOutput, calls=%fused_computation.1 | convolution fusion | flops 12884901888 | bytes 14680064 | tf_op jit(solution)/shard_map/dot_general | solution.py:8
  178.4 0.0 all-reduce.2.cloned.1.call-update
  178.4 49.8 %all-reduce.2.cloned.1.call-done = f32[1024,512]{1,0:T(8,128)} async-done(((f32[1024,512]{1,0:T(8,128)}), f32[1024,512]{1,0:T(8,128)}) %all-reduce.2.cloned.1.call-update) | async-done | bytes 2097168 | tf_op jit(solution)/shard_map/psum | solution.py:15
  228.2 0.0 copy-done
  228.2 1.9 dynamic-slice_multiply_fusion
Async XLA Ops:
  6.5 154.8 %all-gather.2.cloned.1.call-start = ((), (), s32[]{:S(2)}) async-start(), calls=%async_computation | async-start | bytes 10485760 | tf_op jit(solution)/shard_map/all_gather | solution.py:9
  7.3 220.9 %copy-start = (f32[256]{0:T(256)S(1)}, f32[256]{0:T(256)}, u32[]{:S(2)}) copy-start(f32[256]{0:T(256)} %param.5) | copy-start | bytes 3076
  7.3 220.9 %all-reduce.2.cloned.1.call-start = ((), (), s32[]{:S(2)}) async-start(), calls=%async_computation.1 | async-start | bytes 4194304 | tf_op jit(solution)/shard_map/psum | solution.py:15
Sparse Core Ops, SparseCore 0:
  8.9 152.3 all-gather.1
  178.5 49.5 all-reduce.1
where the time goes:
time: 237 us
  waiting for transfers between devices  204 us (86%)
  matrix products  17.1 us (7%)
  between operations  13.4 us (6%)
    all_gather x1, waiting for transfers between devices, body(): lax.all_gather(train_feats, 'query', axis=0, tiled=True)  154 us
    psum x1, waiting for transfers between devices, body(): total = lax.psum(terms, 'proj')  49.8 us
    dot_general x1, matrix products, body(): lax.dot_general(lax.all_gather(train_feats, 'query', axis=0, tiled=True),...  17.1 us
  transfers between devices with their start and end apart: 2, of which 2 were waited for; matrix products, arithmetic and copies ran while one was open for 0% of the time, Pallas kernels for 0%

commit v1 on v0

v1 whole, which is shorter than its diff:
```python
import functools
import jax
import jax.numpy as jnp
from jax import lax
from jax.sharding import PartitionSpec as P
import jax.experimental.pallas as pl
import jax.experimental.pallas.tpu as pltpu

MESH = pl.DeviceIdType.MESH
INWARD = 896
CHUNKS = 8


def split(values):
    high = values.astype(jnp.bfloat16)
    return high, (values - high.astype(jnp.float32)).astype(jnp.bfloat16)


def product(rows, high, low):
    dims = (((1,), (1,)), ((), ()))
    rows_high, rows_low = split(rows)
    count = rows.shape[0]
    first = lax.dot_general(
        jnp.concatenate([rows_high, rows_low], axis=0), high, dims, preferred_element_type=jnp.float32
    )
    second = lax.dot_general(rows_high, low, dims, preferred_element_type=jnp.float32)
    return first[:count] + (first[count:] + second)


def kernel(
    inward, chunks, q_ref, t_ref, o_ref,
    train, query, query_in, high, low, high_in, low_in, partial, taken, sums, sums_taken,
    local_sem, train_recv, query_recv, part_recv, sums_recv, in_send, out_send, query_send, part_send, sums_send,
):
    g, z, p = lax.axis_index("groups"), lax.axis_index("query"), lax.axis_index("proj")
    count = t_ref.shape[0] // chunks
    depth = t_ref.shape[1]
    queries = q_ref.shape[0]
    is_end = jnp.logical_or(z == 0, z == 3)
    is_mid = jnp.logical_not(is_end)
    beside = jnp.where(z == 0, 1, 2)
    across = 3 - z
    end = jnp.where(z == 1, 0, 3)
    far = 3 - end
    outer = pl.ds(inward, depth - inward)
    inner = pl.ds(0, inward)

    def rows_of(j):
        return pl.ds(pl.multiple_of(j * count, count), count)

    def send(src, dst, send_sem, recv_sem, to_z, to_p):
        return pltpu.make_async_remote_copy(
            src_ref=src, dst_ref=dst, send_sem=send_sem, recv_sem=recv_sem,
            device_id=(g, to_z, to_p), device_id_type=MESH,
        )

    def own_in(j, to_z):
        rows = rows_of(j)
        return send(t_ref.at[rows], train.at[z, rows], in_send.at[0, j], train_recv.at[z, j], to_z, p)

    def pass_in(j):
        rows = rows_of(j)
        return send(train.at[end, rows], train.at[end, rows], in_send.at[1, j], train_recv.at[end, j], across, p)

    def own_out(j):
        rows = rows_of(j)
        return send(t_ref.at[rows, outer], train.at[z, rows, outer], out_send.at[0, j], train_recv.at[z, j], end, p)

    def pass_out(j, block, k):
        part = train.at[block, rows_of(j), outer]
        return send(part, part, out_send.at[k, j], train_recv.at[block, j], end, p)

    def query_copy(to_z):
        return send(q_ref.at[:, inner], query_in, query_send.at[0], query_recv.at[0], to_z, p)

    def part_copy(j, half, block):
        rows = rows_of(j)
        return send(
            partial.at[half, block, rows], taken.at[p, half, rows],
            part_send.at[block, half, j], part_recv.at[p, half, j], z, block,
        )

    def part_wait(j, half, peer):
        dst = taken.at[peer, half, rows_of(j)]
        send(dst, dst, part_send.at[0, half, j], part_recv.at[peer, half, j], z, peer).wait_recv()

    def sums_copy(j, to_z):
        rows = rows_of(j)
        return send(sums.at[rows], sums_taken.at[rows], sums_send.at[j], sums_recv.at[j], to_z, p)

    def loop(body):
        def step(j, carry):
            body(j)
            return carry
        lax.fori_loop(0, chunks, step, 0)

    def send_parts(j, half, blocks):
        for block in blocks:
            @pl.when(p != block)
            def _():
                part_copy(j, half, block).start()

    def multiply(j, half, blocks, columns, by_high, by_low):
        rows = rows_of(j)
        result = product(
            jnp.concatenate([train[block, rows, columns] for block in blocks], axis=0), by_high, by_low
        )
        for k, block in enumerate(blocks):
            partial[half, block, rows] = result[k * count:(k + 1) * count]
        send_parts(j, half, blocks)

    def reduced(j, half):
        rows = rows_of(j)
        total = partial[half, p, rows]
        for step in range(1, 4):
            peer = lax.rem(p + step, 4)
            part_wait(j, half, peer)
            total = total + taken[peer, half, rows]
        return total

    own_train = pltpu.make_async_copy(t_ref, train.at[z], local_sem.at[0])
    own_query = pltpu.make_async_copy(q_ref, query, local_sem.at[1])
    own_train.start()
    own_query.start()

    barrier = pltpu.get_barrier_semaphore()
    for step in range(1, 4):
        pl.semaphore_signal(barrier, inc=1, device_id=(g, z, lax.rem(p + step, 4)), device_id_type=MESH)

    @pl.when(is_end)
    def _():
        pl.semaphore_signal(barrier, inc=1, device_id=(g, beside, p), device_id_type=MESH)
        pl.semaphore_wait(barrier, 4)

    @pl.when(is_mid)
    def _():
        pl.semaphore_signal(barrier, inc=1, device_id=(g, across, p), device_id_type=MESH)
        pl.semaphore_signal(barrier, inc=1, device_id=(g, end, p), device_id_type=MESH)
        pl.semaphore_wait(barrier, 5)

    @pl.when(is_end)
    def _():
        query_copy(beside).start()
        loop(lambda j: own_in(j, beside).start())

    @pl.when(is_mid)
    def _():
        def begin(j):
            own_in(j, across).start()
            own_out(j).start()
        loop(begin)

    own_train.wait()
    own_query.wait()

    def split_query(j):
        size = queries // chunks
        rows = pl.ds(pl.multiple_of(j * size, size), size)
        high[rows], low[rows] = split(query[rows])
    loop(split_query)

    @pl.when(is_mid)
    def _():
        def early(j):
            own_in_wait = send(
                train.at[across, rows_of(j)], train.at[across, rows_of(j)],
                in_send.at[0, j], train_recv.at[across, j], across, p,
            )
            own_in_wait.wait_recv()
            pass_out(j, across, 1).start()
            multiply(j, 0, (1, 2), slice(None), high[...], low[...])
        loop(early)

        def late(j):
            pass_in(j).wait_recv()
            pass_in(j).start()
            rows = rows_of(j)
            send(
                train.at[far, rows], train.at[far, rows], in_send.at[1, j], train_recv.at[far, j], across, p
            ).wait_recv()
            pass_out(j, far, 2).start()

            @pl.when(j == 0)
            def _():
                query_copy(end).wait_recv()

                def split_in(k):
                    size = queries // chunks
                    some = pl.ds(pl.multiple_of(k * size, size), size)
                    high_in[some], low_in[some] = split(query_in[some])
                loop(split_in)

            multiply(j, 1, (0, 1, 2, 3), slice(0, inward), high_in[...], low_in[...])
            multiply(j, 0, (0, 3), slice(None), high[...], low[...])

            @pl.when(j > 0)
            def _():
                finish(j - 1)

        def finish(j):
            rows = rows_of(j)
            sums[rows] = reduced(j, 1)
            sums_copy(j, end).start()
            o_ref[rows] = reduced(j, 0)

        loop(late)
        finish(chunks - 1)

        def drain(j):
            own_in(j, across).wait_send()
            pass_in(j).wait_send()
            own_out(j).wait_send()
            pass_out(j, across, 1).wait_send()
            pass_out(j, far, 2).wait_send()
            sums_copy(j, end).wait_send()
            for half in (0, 1):
                for block in range(4):
                    @pl.when(p != block)
                    def _():
                        part_copy(j, half, block).wait_send()
        loop(drain)

    @pl.when(is_end)
    def _():
        def wait_train(j, block):
            part = train.at[block, rows_of(j), outer]
            send(part, part, in_send.at[0, j], train_recv.at[block, j], beside, p).wait_recv()

        def early(j):
            wait_train(j, 1)
            wait_train(j, 2)
            multiply(j, 0, (1, 2), slice(inward, depth), high[:, inward:], low[:, inward:])
        loop(early)

        def late(j):
            wait_train(j, across)
            multiply(j, 0, (0, 3), slice(inward, depth), high[:, inward:], low[:, inward:])
        loop(late)

        def finish(j):
            rows = rows_of(j)
            total = reduced(j, 0)
            sums_copy(j, beside).wait_recv()
            o_ref[rows] = total + sums_taken[rows]
        loop(finish)

        query_copy(beside).wait_send()

        def drain(j):
            own_in(j, beside).wait_send()
            for block in range(4):
                @pl.when(p != block)
                def _():
                    part_copy(j, 0, block).wait_send()
        loop(drain)


def line_of_four(query_feats, train_feats, out_weight):
    queries, depth = query_feats.shape
    rows = train_feats.shape[0]
    inward = min(INWARD, depth // 2)
    f32, bf16 = jnp.float32, jnp.bfloat16
    dma = pltpu.SemaphoreType.DMA
    sums = pl.pallas_call(
        functools.partial(kernel, inward, CHUNKS),
        out_shape=jax.ShapeDtypeStruct((rows, queries), f32),
        in_specs=[pl.BlockSpec(memory_space=pl.ANY)] * 2,
        out_specs=pl.BlockSpec(memory_space=pltpu.VMEM),
        scratch_shapes=[
            pltpu.VMEM((4, rows, depth), f32),
            pltpu.VMEM((queries, depth), f32),
            pltpu.VMEM((queries, inward), f32),
            pltpu.VMEM((queries, depth), bf16),
            pltpu.VMEM((queries, depth), bf16),
            pltpu.VMEM((queries, inward), bf16),
            pltpu.VMEM((queries, inward), bf16),
            pltpu.VMEM((2, 4, rows, queries), f32),
            pltpu.VMEM((4, 2, rows, queries), f32),
            pltpu.VMEM((rows, queries), f32),
            pltpu.VMEM((rows, queries), f32),
            dma((2,)),
            dma((4, CHUNKS)),
            dma((1,)),
            dma((4, 2, CHUNKS)),
            dma((CHUNKS,)),
            dma((2, CHUNKS)),
            dma((3, CHUNKS)),
            dma((1,)),
            dma((4, 2, CHUNKS)),
            dma((CHUNKS,)),
        ],
        compiler_params=pltpu.CompilerParams(
            collective_id=0, has_side_effects=True, vmem_limit_bytes=56 << 20
        ),
        cost_estimate=pl.CostEstimate(
            flops=3 * 2 * 4 * rows * queries * depth, bytes_accessed=4 * (rows + queries) * depth, transcendentals=0
        ),
    )(query_feats, train_feats)
    return sums * out_weight[:, None]


def any_mesh(query_feats, train_feats, out_weight):
    terms = lax.dot_general(
        lax.all_gather(train_feats, "query", axis=0, tiled=True),
        query_feats,
        (((1,), (1,)), ((), ())),
        precision=lax.Precision.HIGHEST,
        preferred_element_type=jnp.float32,
    )
    return lax.psum_scatter(terms, "proj", scatter_dimension=0, tiled=True) * out_weight[:, None]


def solution(mesh):
    placed = (P(("groups", "query"), "proj"), P(("groups", "query"), "proj"), P(("groups", "proj")))
    body = line_of_four if mesh.shape["query"] == mesh.shape["proj"] == 4 else any_mesh
    return jax.shard_map(
        body, mesh=mesh, in_specs=placed, out_specs=P(("groups", "proj"), "query"), check_vma=False
    )
```

time: 237 us -> 130 us (0.55)
  waiting for transfers between devices: 204 us -> 0 us
  Pallas kernels: 0 us -> 128 us
  matrix products: 17.1 us -> 0 us
  between operations: 13.4 us -> 0.02 us
    all_gather x1 -> x0, waiting for transfers between devices: 154 us -> none  [body(): lax.all_gather(train_feats, 'query', axis=0, tiled=True)]
    pallas_call x0 -> x1, Pallas kernels: none -> 128 us  [line_of_four(): pl.pallas_call(functools.partial(kernel, inward, CHUNKS), out_shape=jax.S...]
    psum x1 -> x0, waiting for transfers between devices: 49.8 us -> none  [body(): total = lax.psum(terms, 'proj')]
    dot_general x1 -> x0, matrix products: 17.1 us -> none  [body(): lax.dot_general(lax.all_gather(train_feats, 'query', axis=0, tiled=True),...]
  transfers between devices with their start and end apart: 2 -> 0, of which waited for: 2 -> 0; matrix products, arithmetic and copies ran while one was open for 0% -> 0% of each run, Pallas kernels for 0% -> 0%
where the time goes in v1:
time: 130 us
  Pallas kernels  128 us (98%)
  other arithmetic  1.94 us (1%)
    pallas_call x1, Pallas kernels, line_of_four(): pl.pallas_call(functools.partial(kernel, inward, CHUNKS), out_shape=jax.S...  128 us

profile of v1, /device:TPU:0, one launch (start us, length us, event | category | flops | bytes accessed | tf_op | source)
XLA Modules:
  0.0 129.7 jit_solution(11024887309419995366)
XLA Ops:
  0.0 0.0 copy-start
  0.0 127.8 %shard_map.37 = f32[256,512]{1,0:T(8,128)} custom-call(f32[512,2048]{1,0:T(8,128)} %q_ref.1, f32[256,2048]{1,0:T(8,128)} %t_ref.1), custom_call_target="tpu_custom_call" | custom-call | flops 6442450944 | bytes 6291456 | tf_op jit(solution)/shard_map/pallas_call | solution.py:264
  127.8 0.0 copy-done
  127.8 1.9 %broadcast_multiply_fusion = f32[256,512]{1,0:T(8,128)} fusion(f32[256,512]{1,0:T(8,128)} %shard_map.37, f32[256]{0:T(256)S(1)} %copy-done), kind=kLoop, calls=%fused_computation | loop fusion | flops 131072 | bytes 1049600 | tf_op jit(solution)/shard_map/mul | solution.py:299
Async XLA Ops:
  0.0 127.8 %copy-start = (f32[256]{0:T(256)S(1)}, f32[256]{0:T(256)}, u32[]{:S(2)}) copy-start(f32[256]{0:T(256)} %param.5) | copy-start | bytes 3076

commit v2 on v1

v2 whole, which is shorter than its diff:
```python
import functools
import jax
import jax.numpy as jnp
from jax import lax
from jax.sharding import PartitionSpec as P
import jax.experimental.pallas as pl
import jax.experimental.pallas.tpu as pltpu

MESH = pl.DeviceIdType.MESH
INWARD = 768
CHUNKS = 16
GROUPS = 8


def split(values):
    high = values.astype(jnp.bfloat16)
    return high, (values - high.astype(jnp.float32)).astype(jnp.bfloat16)


def product(rows, high, low):
    dims = (((1,), (0,)), ((), ()))
    rows_high, rows_low = split(rows)
    count = rows.shape[0]
    first = lax.dot_general(
        jnp.concatenate([rows_high, rows_low], axis=0), high, dims, preferred_element_type=jnp.float32
    )
    second = lax.dot_general(rows_high, low, dims, preferred_element_type=jnp.float32)
    return first[:count] + (first[count:] + second)


def kernel(
    inward, chunks, groups, q_ref, t_ref, o_ref,
    train, query, query_in, high, low, high_in, low_in, partial, taken, sums, sums_taken,
    local_sem, train_recv, query_recv, part_recv, sums_recv, in_send, out_send, query_send, part_send, sums_send,
):
    g, z, p = lax.axis_index("groups"), lax.axis_index("query"), lax.axis_index("proj")
    count = t_ref.shape[0] // chunks
    depth = t_ref.shape[1]
    queries = q_ref.shape[0]
    is_end = jnp.logical_or(z == 0, z == 3)
    is_mid = jnp.logical_not(is_end)
    beside = jnp.where(z == 0, 1, 2)
    across = 3 - z
    end = jnp.where(z == 1, 0, 3)
    far = 3 - end
    outer = pl.ds(inward, depth - inward)
    inner = pl.ds(0, inward)

    def rows_of(j):
        return pl.ds(pl.multiple_of(j * count, count), count)

    def group_rows(s):
        size = t_ref.shape[0] // groups
        return pl.ds(pl.multiple_of(s * size, size), size)

    def send(src, dst, send_sem, recv_sem, to_z, to_p):
        return pltpu.make_async_remote_copy(
            src_ref=src, dst_ref=dst, send_sem=send_sem, recv_sem=recv_sem,
            device_id=(g, to_z, to_p), device_id_type=MESH,
        )

    def own_in(j, to_z):
        rows = rows_of(j)
        return send(t_ref.at[rows], train.at[z, rows], in_send.at[0, j], train_recv.at[z, j], to_z, p)

    def pass_in(j):
        rows = rows_of(j)
        return send(train.at[end, rows], train.at[end, rows], in_send.at[1, j], train_recv.at[end, j], across, p)

    def own_out(j):
        rows = rows_of(j)
        return send(t_ref.at[rows, outer], train.at[z, rows, outer], out_send.at[0, j], train_recv.at[z, j], end, p)

    def pass_out(j, block, k):
        part = train.at[block, rows_of(j), outer]
        return send(part, part, out_send.at[k, j], train_recv.at[block, j], end, p)

    def query_copy(to_z):
        return send(q_ref.at[:, inner], query_in, query_send.at[0], query_recv.at[0], to_z, p)

    def part_copy(j, half, block):
        rows = group_rows(j)
        return send(
            partial.at[half, block, rows], taken.at[p, half, rows],
            part_send.at[block, half, j], part_recv.at[p, half, j], z, block,
        )

    def part_wait(j, half, peer):
        dst = taken.at[peer, half, group_rows(j)]
        send(dst, dst, part_send.at[0, half, j], part_recv.at[peer, half, j], z, peer).wait_recv()

    def sums_copy(j, to_z):
        rows = group_rows(j)
        return send(sums.at[rows], sums_taken.at[rows], sums_send.at[j], sums_recv.at[j], to_z, p)

    def loop(body, low=0, high=chunks):
        def step(j, carry):
            body(j)
            return carry
        lax.fori_loop(low, high, step, 0)

    def multiply(first, number, half, blocks, columns, by_high, by_low):
        rows = pl.ds(pl.multiple_of(first, number), number)
        result = product(
            jnp.concatenate([train[block, rows, columns] for block in blocks], axis=0), by_high, by_low
        )
        for k, block in enumerate(blocks):
            partial[half, block, rows] = result[k * number:(k + 1) * number]

    def send_parts(s, half, block):
        @pl.when(p != block)
        def _():
            part_copy(s, half, block).start()

    def reduced(s, half):
        rows = group_rows(s)
        total = partial[half, p, rows]
        for step in range(1, 4):
            peer = lax.rem(p + step, 4)
            part_wait(s, half, peer)
            total = total + taken[peer, half, rows]
        return total

    def split_query(src, into_high, into_low):
        size = 128
        def step(k):
            some = pl.ds(pl.multiple_of(k * size, size), size)
            into_high[:, some], into_low[:, some] = split(src[some].T)
        loop(step, 0, queries // size)

    own_train = pltpu.make_async_copy(t_ref, train.at[z], local_sem.at[0])
    own_query = pltpu.make_async_copy(q_ref, query, local_sem.at[1])
    own_train.start()
    own_query.start()

    barrier = pltpu.get_barrier_semaphore()
    for step in range(1, 4):
        pl.semaphore_signal(barrier, inc=1, device_id=(g, z, lax.rem(p + step, 4)), device_id_type=MESH)

    @pl.when(is_end)
    def _():
        pl.semaphore_signal(barrier, inc=1, device_id=(g, beside, p), device_id_type=MESH)
        pl.semaphore_wait(barrier, 4)

    @pl.when(is_mid)
    def _():
        pl.semaphore_signal(barrier, inc=1, device_id=(g, across, p), device_id_type=MESH)
        pl.semaphore_signal(barrier, inc=1, device_id=(g, end, p), device_id_type=MESH)
        pl.semaphore_wait(barrier, 5)

    @pl.when(is_end)
    def _():
        query_copy(beside).start()
        loop(lambda j: own_in(j, beside).start())

    @pl.when(is_mid)
    def _():
        def begin(j):
            own_in(j, across).start()
            own_out(j).start()
        loop(begin)

    own_train.wait()
    own_query.wait()
    split_query(query, high, low)
    all_rows = t_ref.shape[0]
    per = chunks // groups
    size = all_rows // groups

    def send_all(half, block):
        loop(lambda s: send_parts(s, half, block), 0, groups)

    @pl.when(is_mid)
    def _():
        def wait_train(j, block):
            part = train.at[block, rows_of(j)]
            send(part, part, in_send.at[0, j], train_recv.at[block, j], across, p).wait_recv()

        def take_across(s):
            for k in range(per):
                wait_train(s * per + k, across)
                pass_out(s * per + k, across, 1).start()

        def take_end(s):
            for k in range(per):
                wait_train(s * per + k, end)
                pass_in(s * per + k).start()

        def take_far(s):
            for k in range(per):
                wait_train(s * per + k, far)
                pass_out(s * per + k, far, 2).start()

        def whole(s, block):
            multiply(s * size, size, 0, (block,), slice(None), high[...], low[...])
            send_parts(s, 0, block)

        def inward_part(s, block):
            multiply(s * size, size, 1, (block,), slice(0, inward), high_in[...], low_in[...])
            send_parts(s, 1, block)

        multiply(0, all_rows, 0, (z,), slice(None), high[...], low[...])
        send_all(0, z)

        def early(s):
            take_across(s)

            @pl.when(s == groups - 1)
            def _():
                take_end(0)

            whole(s, across)
        loop(early, 0, groups)

        query_copy(end).wait_recv()
        split_query(query_in, high_in, low_in)
        multiply(0, all_rows, 1, (1, 2), slice(0, inward), high_in[...], low_in[...])
        send_all(1, 1)
        send_all(1, 2)

        def finish(s):
            rows = group_rows(s)
            sums[rows] = reduced(s, 1)
            sums_copy(s, end).start()
            o_ref[rows] = reduced(s, 0)

        def late(s):
            @pl.when(s < groups - 1)
            def _():
                take_end(s + 1)

            def one(k):
                block = jnp.where(k == 0, end, far)

                @pl.when(k == 1)
                def _():
                    take_far(s)

                inward_part(s, block)
                whole(s, block)
            loop(one, 0, 2)

            @pl.when(s > 0)
            def _():
                finish(s - 1)
        loop(late, 0, groups)
        finish(groups - 1)

        def drain(j):
            own_in(j, across).wait_send()
            pass_in(j).wait_send()
            own_out(j).wait_send()
            pass_out(j, across, 1).wait_send()
            pass_out(j, far, 2).wait_send()
        loop(drain)

        def drain_parts(s):
            sums_copy(s, end).wait_send()
            for half in (0, 1):
                for block in range(4):
                    @pl.when(p != block)
                    def _():
                        part_copy(s, half, block).wait_send()
        loop(drain_parts, 0, groups)

    @pl.when(is_end)
    def _():
        columns = slice(inward, depth)

        def wait_train(s, block):
            for k in range(per):
                part = train.at[block, rows_of(s * per + k), outer]
                send(part, part, in_send.at[0, 0], train_recv.at[block, s * per + k], beside, p).wait_recv()

        multiply(0, all_rows, 0, (z,), columns, high[inward:], low[inward:])
        send_all(0, z)

        def early(s):
            wait_train(s, 1)
            wait_train(s, 2)
            multiply(s * size, size, 0, (1, 2), columns, high[inward:], low[inward:])
            send_parts(s, 0, 1)
            send_parts(s, 0, 2)
        loop(early, 0, groups)

        def late(s):
            wait_train(s, across)
            multiply(s * size, size, 0, (across,), columns, high[inward:], low[inward:])
            send_parts(s, 0, across)
        loop(late, 0, groups)

        def finish(s):
            rows = group_rows(s)
            o_ref[rows] = reduced(s, 0)
        loop(finish, 0, groups)

        def add_sums(s):
            rows = group_rows(s)
            sums_copy(s, beside).wait_recv()
            o_ref[rows] = o_ref[rows] + sums_taken[rows]
        loop(add_sums, 0, groups)

        query_copy(beside).wait_send()
        loop(lambda j: own_in(j, beside).wait_send())

        def drain_parts(s):
            for block in range(4):
                @pl.when(p != block)
                def _():
                    part_copy(s, 0, block).wait_send()
        loop(drain_parts, 0, groups)


def line_of_four(query_feats, train_feats, out_weight):
    queries, depth = query_feats.shape
    rows = train_feats.shape[0]
    inward = min(INWARD, depth // 2)
    f32, bf16 = jnp.float32, jnp.bfloat16
    dma = pltpu.SemaphoreType.DMA
    sums = pl.pallas_call(
        functools.partial(kernel, inward, CHUNKS, GROUPS),
        out_shape=jax.ShapeDtypeStruct((rows, queries), f32),
        in_specs=[pl.BlockSpec(memory_space=pl.ANY)] * 2,
        out_specs=pl.BlockSpec(memory_space=pltpu.VMEM),
        scratch_shapes=[
            pltpu.VMEM((4, rows, depth), f32),
            pltpu.VMEM((queries, depth), f32),
            pltpu.VMEM((queries, inward), f32),
            pltpu.VMEM((depth, queries), bf16),
            pltpu.VMEM((depth, queries), bf16),
            pltpu.VMEM((inward, queries), bf16),
            pltpu.VMEM((inward, queries), bf16),
            pltpu.VMEM((2, 4, rows, queries), f32),
            pltpu.VMEM((4, 2, rows, queries), f32),
            pltpu.VMEM((rows, queries), f32),
            pltpu.VMEM((rows, queries), f32),
            dma((2,)),
            dma((4, CHUNKS)),
            dma((1,)),
            dma((4, 2, GROUPS)),
            dma((GROUPS,)),
            dma((2, CHUNKS)),
            dma((3, CHUNKS)),
            dma((1,)),
            dma((4, 2, GROUPS)),
            dma((GROUPS,)),
        ],
        compiler_params=pltpu.CompilerParams(
            collective_id=0, has_side_effects=True, vmem_limit_bytes=56 << 20
        ),
        cost_estimate=pl.CostEstimate(
            flops=3 * 2 * 4 * rows * queries * depth, bytes_accessed=4 * (rows + queries) * depth, transcendentals=0
        ),
    )(query_feats, train_feats)
    return sums * out_weight[:, None]


def any_mesh(query_feats, train_feats, out_weight):
    terms = lax.dot_general(
        lax.all_gather(train_feats, "query", axis=0, tiled=True),
        query_feats,
        (((1,), (1,)), ((), ())),
        precision=lax.Precision.HIGHEST,
        preferred_element_type=jnp.float32,
    )
    return lax.psum_scatter(terms, "proj", scatter_dimension=0, tiled=True) * out_weight[:, None]


def solution(mesh):
    placed = (P(("groups", "query"), "proj"), P(("groups", "query"), "proj"), P(("groups", "proj")))
    body = line_of_four if mesh.shape["query"] == mesh.shape["proj"] == 4 else any_mesh
    return jax.shard_map(
        body, mesh=mesh, in_specs=placed, out_specs=P(("groups", "proj"), "query"), check_vma=False
    )
```

time: 130 us -> 109 us (0.84)
  Pallas kernels: 128 us -> 107 us
    pallas_call x1, Pallas kernels: 128 us -> 107 us  [line_of_four(): pl.pallas_call(functools.partial(kernel, inward, CHUNKS, GROUPS), out_sha...]
where the time goes in v2:
time: 109 us
  Pallas kernels  107 us (98%)
  other arithmetic  1.94 us (2%)
    pallas_call x1, Pallas kernels, line_of_four(): pl.pallas_call(functools.partial(kernel, inward, CHUNKS, GROUPS), out_sha...  107 us

profile of v2, /device:TPU:0, one launch (start us, length us, event | category | flops | bytes accessed | tf_op | source)
XLA Modules:
  0.0 109.3 jit_solution(15731491047762400294)
XLA Ops:
  0.0 0.0 copy-start
  0.0 107.4 %shard_map.37 = f32[256,512]{1,0:T(8,128)} custom-call(f32[512,2048]{1,0:T(8,128)} %q_ref.1, f32[256,2048]{1,0:T(8,128)} %t_ref.1), custom_call_target="tpu_custom_call" | custom-call | flops 6442450944 | bytes 6291456 | tf_op jit(solution)/shard_map/pallas_call | solution.py:320
  107.4 0.0 copy-done
  107.4 1.9 %broadcast_multiply_fusion = f32[256,512]{1,0:T(8,128)} fusion(f32[256,512]{1,0:T(8,128)} %shard_map.37, f32[256]{0:T(256)S(1)} %copy-done), kind=kLoop, calls=%fused_computation | loop fusion | flops 131072 | bytes 1049600 | tf_op jit(solution)/shard_map/mul | solution.py:355
Async XLA Ops:
  0.0 107.4 %copy-start = (f32[256]{0:T(256)S(1)}, f32[256]{0:T(256)}, u32[]{:S(2)}) copy-start(f32[256]{0:T(256)} %param.5) | copy-start | bytes 3076

commit v3 on v2

--- a/solution.py
+++ b/solution.py
@@ -203,6 +203,11 @@
         send_all(0, z)
 
         def early(s):
+            @pl.when(s == groups - 1)
+            def _():
+                query_copy(end).wait_recv()
+                split_query(query_in, high_in, low_in)
+
             take_across(s)
 
             @pl.when(s == groups - 1)
@@ -212,8 +217,6 @@
             whole(s, across)
         loop(early, 0, groups)
 
-        query_copy(end).wait_recv()
-        split_query(query_in, high_in, low_in)
         multiply(0, all_rows, 1, (1, 2), slice(0, inward), high_in[...], low_in[...])
         send_all(1, 1)
         send_all(1, 2)

time: 109 us -> 109 us (level)
  no operation moved by 1% of the time
where the time goes in v3:
time: 109 us
  Pallas kernels  107 us (98%)
  other arithmetic  1.94 us (2%)
    pallas_call x1, Pallas kernels, line_of_four(): pl.pallas_call(functools.partial(kernel, inward, CHUNKS, GROUPS), out_sha...  107 us

profile of v3, /device:TPU:0, one launch (start us, length us, event | category | flops | bytes accessed | tf_op | source)
XLA Modules:
  0.0 109.3 jit_solution(6964928132916007678)
XLA Ops:
  0.0 0.0 copy-start
  0.0 107.3 %shard_map.37 = f32[256,512]{1,0:T(8,128)} custom-call(f32[512,2048]{1,0:T(8,128)} %q_ref.1, f32[256,2048]{1,0:T(8,128)} %t_ref.1), custom_call_target="tpu_custom_call" | custom-call | flops 6442450944 | bytes 6291456 | tf_op jit(solution)/shard_map/pallas_call | solution.py:323
  107.3 0.0 copy-done
  107.4 1.9 %broadcast_multiply_fusion = f32[256,512]{1,0:T(8,128)} fusion(f32[256,512]{1,0:T(8,128)} %shard_map.37, f32[256]{0:T(256)S(1)} %copy-done), kind=kLoop, calls=%fused_computation | loop fusion | flops 131072 | bytes 1049600 | tf_op jit(solution)/shard_map/mul | solution.py:358
Async XLA Ops:
  0.0 107.3 %copy-start = (f32[256]{0:T(256)S(1)}, f32[256]{0:T(256)}, u32[]{:S(2)}) copy-start(f32[256]{0:T(256)} %param.5) | copy-start | bytes 3076
